TPU v7x, 512 devices: a whole 4x8x8 slice. The times are simulated.
512 devices in a mesh: dp: 16 (over y, core), expert: 32 (over z, x).
Axes of the slice: x: 4, y: 8, z: 8, core: 2. Of those that a mesh axis runs over, the one named last changes fastest.
Arguments:
- stream_q: bfloat16 [4096, 4096], P('dp', 'expert'), may hold values from -6 to 6
- stream_k: bfloat16 [4096, 4096], P('dp', 'expert'), may hold values from -6 to 6
- stream_v: bfloat16 [4096, 4096], P('dp', 'expert'), may hold values from -6 to 6
- conv_taps: float32 [3, 3, 4096], P(None, None, 'expert'), may hold values from -14 to 14
- norm_gain: bfloat16 [4096], P('expert'), may hold values from 0.3984375 to 1.59375
- slot_token: int32 [16, 384], P('dp'), may hold values from 0 to 256, as said below
- expert_count: int32 [16, 2], P('dp'), may hold values from 0 to 256, as said below
- route_prob: float32 [4096], P('dp'), may hold values from 0.25 to 1
- w_proj: bfloat16 [4096, 2, 8192], P('dp', None, 'expert'), may hold values from -0.09375 to 0.09375
- grad_out: bfloat16 [4096, 8192], P('dp', 'expert'), may hold values from -0.75 to 0.75
Outputs:
- activation: bfloat16 [4096, 8192], P('dp', 'expert')
- weight_grad: float32 [4096, 2, 8192], P('dp', None, 'expert')
Inputs may be any that keep to these rules, and one draw needn't show every extreme that they name: `slot_token`: for each index of dp the slots hold its 256 local token numbers, each exactly once, grouped by expert in expert order; each group starts at a multiple of 128 and is padded with the value 256 up to a multiple of 128; all slots after the last group hold 256. `expert_count`: the size of each expert's group in slot_token, before padding; each row sums to 256.
All inputs are finite; a program needn't handle non-finite values.
Results may differ from a plain program's by a relative error of at most 0.023.
Values may be sent and summed in bfloat16 or wider, within the bound.
No kernel may reach another device: no remote copies, remote signals or barrier semaphores. Data moves between devices by JAX's collectives and lax.ppermute only.
A program may use at most 64 MiB of HBM per device.

v0:
```python
import jax
import jax.numpy as jnp
from jax import lax
from jax.sharding import PartitionSpec as P

D = 4096
BLOCK = 128
epsilon = 1e-06


def from_behind(value, axis, steps):
    count = lax.axis_size(axis)
    leading, last = (max(0, -steps), min(count, count - steps))
    return lax.ppermute(value, axis, [(source, source + steps) for source in range(leading, last)])


def block_owner(counts, num_blocks):
    padded = (counts + BLOCK - 1) // BLOCK * BLOCK
    ends = jnp.cumsum(padded)
    starts = jnp.arange(num_blocks, dtype=jnp.int32) * BLOCK
    owner = jnp.sum((starts[:, None] >= ends[None, :]).astype(jnp.int32), axis=1)
    return jnp.minimum(owner, counts.shape[0] - 1)


def on_device(
    stream_q,
    stream_k,
    stream_v,
    conv_taps,
    norm_gain,
    slot_token,
    expert_count,
    route_prob,
    w_proj,
    grad_out,
):
    stacked = jnp.stack([stream_q, stream_k, stream_v])
    before = from_behind(stacked[:, -2:, :], "dp", 1)
    extended = jnp.concatenate([before, stacked], axis=1).astype(jnp.float32)
    convolved = (
        conv_taps[:, 0, None, :] * extended[:, 2:]
        + conv_taps[:, 1, None, :] * extended[:, 1:-1]
        + conv_taps[:, 2, None, :] * extended[:, :-2]
    )
    mixed = (convolved[0] * convolved[1] * convolved[2]).astype(jnp.bfloat16)
    mixed_f = mixed.astype(jnp.float32)
    total = lax.psum(jnp.sum(mixed_f * mixed_f, axis=1), "expert")
    inv_rms = lax.rsqrt(total / D + epsilon)
    normed = (mixed_f * inv_rms[:, None] * norm_gain.astype(jnp.float32)).astype(jnp.bfloat16)
    gathered = lax.all_gather(normed, "expert", axis=1, tiled=True)
    tok_count = gathered.shape[0]
    slots = slot_token[0]
    num_blocks = slots.shape[0] // BLOCK
    owner = block_owner(expert_count[0], num_blocks)
    padded_rows = jnp.concatenate(
        [gathered, jnp.zeros((1, gathered.shape[1]), jnp.bfloat16)], axis=0
    )
    x_blocks = padded_rows[slots].reshape(num_blocks, BLOCK, gathered.shape[1])
    hid_local = w_proj.shape[2]
    experts_here = w_proj.shape[1]
    selector = (owner[:, None] == jnp.arange(experts_here, dtype=jnp.int32)[None, :]).astype(
        jnp.bfloat16
    )
    columns = x_blocks
    chosen_w = jnp.einsum(
        "neh,be->bnh",
        lax.all_gather(w_proj, "dp", axis=0, tiled=True),
        selector,
        preferred_element_type=jnp.float32,
    ).astype(jnp.bfloat16)
    pre_act = jnp.einsum("brn,bnh->brh", columns, chosen_w, preferred_element_type=jnp.float32)
    pre_act = pre_act.reshape(num_blocks * BLOCK, hid_local)
    slot_prob = jnp.concatenate([route_prob, jnp.zeros((1,), jnp.float32)])[slots][:, None]
    sigmoid_z = jax.nn.sigmoid(pre_act)
    hidden = (slot_prob * pre_act * sigmoid_z).astype(jnp.bfloat16)
    activation = (
        jnp.zeros((tok_count + 1, hid_local), jnp.bfloat16).at[slots].set(hidden)[:tok_count]
    )
    slot_grad = jnp.concatenate([grad_out, jnp.zeros((1, hid_local), jnp.bfloat16)], axis=0)[
        slots
    ].astype(jnp.float32)
    grad_pre = (slot_grad * slot_prob * sigmoid_z * (1.0 + pre_act * (1.0 - sigmoid_z))).astype(
        jnp.bfloat16
    )
    grad_blocks = grad_pre.reshape(num_blocks, BLOCK, hid_local)
    masked_grad = grad_blocks[None, :, :, :] * selector.T[:, :, None, None]
    columns = x_blocks
    weight_grad = lax.psum_scatter(
        jnp.einsum(
            "brd,ebrh->deh", columns, masked_grad, preferred_element_type=jnp.float32
        ).astype(jnp.bfloat16),
        "dp",
        scatter_dimension=0,
        tiled=True,
    ).astype(jnp.float32)
    return (activation, weight_grad)


def solution(mesh):
    placed = (
        P("dp", "expert"),
        P("dp", "expert"),
        P("dp", "expert"),
        P(None, None, "expert"),
        P("expert"),
        P("dp", None),
        P("dp", None),
        P("dp"),
        P("dp", None, "expert"),
        P("dp", "expert"),
    )
    return jax.shard_map(
        on_device,
        mesh=mesh,
        in_specs=placed,
        out_specs=(P("dp", "expert"), P("dp", None, "expert")),
        check_vma=False,
    )
```

profile of v0, /device:TPU:29, one launch (start us, length us, event | category | flops | bytes accessed | tf_op | source)
XLA Modules:
  0.0 303.6 jit_solution(1994741817525698117)
XLA Ops:
  7.2 0.7 pad_maximum_fusion.1
  8.0 5.0 %collective-permute-start = (bf16[3,2,128]{2,1,0:T(2,128)(2,1)S(1)}, bf16[3,2,128]{2,1,0:T(2,128)(2,1)S(1)}, u32[]{:S(2)}, u32[]{:S(2)}) collective-permute-start(bf16[3,2,128]{2,1,0:T(2,128)(2,1)S(1)} %pad_maximum_fusion.1), channel_id=1, source_target_pairs={{0,32},{32,64},{64,96},{96,128},{128,160},{160,192},{192,224},{224... | collective-permute-start | bytes 4616 | tf_op jit(solution)/shard_map/ppermute | solution.py:14
  12.9 0.8 fusion.29
  13.8 0.7 convert_element_type.59
  14.4 0.9 maximum_convert_fusion
  15.6 62.6 %psum.7 = f32[256]{0:T(256)S(1)} all-reduce(f32[256]{0:T(256)S(1)} %get-tuple-element.10), channel_id=1, replica_groups=mesh['dp'=16,'expert'=32] {'expert'}, use_global_device_ids=true, to_apply=%region_1.0 | all-reduce | flops 256 | bytes 2048 | tf_op jit(solution)/shard_map/psum | solution.py:47
  78.2 0.7 fusion.17
  79.0 0.7 all-gather.5.cloned.1.call-update
  79.8 0.7 pad_maximum_fusion
  80.5 0.7 fusion.24
  81.2 2.8 gather_fusion
  84.0 2.6 gather_fusion.2
  86.6 0.2 reduce-window.8
  86.9 81.5 %all-gather.3.cloned.1.call-done = bf16[256,4096]{1,0:T(8,128)(2,1)} async-done(((bf16[256,128]{1,0:T(8,128)(2,1)}), bf16[256,4096]{1,0:T(8,128)(2,1)}) %all-gather.3.cloned.1.call-update) | async-done | bytes 2097168 | tf_op jit(solution)/shard_map/all_gather | solution.py:50
  168.4 1.8 concatenate.14
  170.1 4.1 %gather_fusion.1 = bf16[384,4096]{1,0:T(8,128)(2,1)} fusion(bf16[257,4096]{1,0:T(8,128)(2,1)S(1)} %concatenate.14, s32[1024]{0:T(1024)S(1)} %pad_clamp_fusion), kind=kCustom, calls=%fused_computation.1 | custom fusion | bytes 6292992 | tf_op jit(solution)/shard_map/gather | solution.py:58
  174.2 42.7 %all-gather.5.cloned.1.call-done = bf16[4096,2,256]{2,1,0:T(2,128)(2,1)} async-done(((bf16[256,2,256]{2,1,0:T(2,128)(2,1)}), bf16[4096,2,256]{2,1,0:T(2,128)(2,1)}) %all-gather.5.cloned.1.call-update) | async-done | bytes 4194320 | tf_op jit(solution)/shard_map/all_gather | solution.py:67
  217.0 7.5 %convolution_convert_fusion = bf16[3,4096,256]{2,0,1:T(4,128)(2,1)S(1)} fusion(bf16[4096,2,256]{2,1,0:T(2,128)(2,1)} %all-gather.5.cloned.1.call-done, s32[3]{0:T(128)S(1)} %broadcast_minimum_fusion), kind=kOutput, calls=%fused_computation.5 | convolution fusion | flops 15728646 | bytes 10485772 | tf_op jit(solution)/shard_map/neh,be->bnh/dot_general | solution.py:65
  224.5 1.3 fusion.6
  225.8 4.4 %bitcast_convert_fusion = bf16[4096,2,256]{2,0,1:T(8,128)(2,1)} fusion(bf16[3,128,4096,1]{2,1,0,3:T(8,128)(2,1)S(1)} %bitcast.50, bf16[2,3]{1,0:T(2,128)(2,1)S(1)} %compare_convert_fusion, bf16[3,128,256]{2,1,0:T(8,128)(2,1)S(1)} %get-tuple-element.15), kind=kOutput, calls=%fused_computation.4 | convolution fusion | flops 1613496320 | bytes 7536652 | tf_op jit(solution)/shard_map/brd,ebrh->deh/dot_general | solution.py:89
  230.3 1.9 scatter_custom_fusion
  232.2 0.7 slice.56
  232.8 62.2 %reduce-scatter.2.cloned.1.call-done = bf16[256,2,256]{2,0,1:T(8,128)(2,1)} async-done(((bf16[4096,2,256]{2,0,1:T(8,128)(2,1)}), bf16[256,2,256]{2,0,1:T(8,128)(2,1)}) %reduce-scatter.2.cloned.1.call-update) | async-done | bytes 262160 | tf_op jit(solution)/shard_map/reduce_scatter | solution.py:88
  295.1 2.0 copy.21
  (27 shorter events, 0.7 us)
Async XLA Ops:
  7.2 76.8 %copy-start.2 = (bf16[256,256]{1,0:T(8,128)(2,1)S(1)}, bf16[256,256]{1,0:T(8,128)(2,1)}, u32[]{:S(2)}) copy-start(bf16[256,256]{1,0:T(8,128)(2,1)} %param.19) | copy-start | bytes 393220
  7.2 79.4 %copy-start.3 = (s32[1,2]{1,0:T(1,128)S(1)}, s32[1,2]{1,0:T(1,128)}, u32[]{:S(2)}) copy-start(s32[1,2]{1,0:T(1,128)} %param.16) | copy-start | bytes 28
  7.2 161.2 %all-gather.3.cloned.1.call-start = ((), (), s32[]{:S(2)}) async-start(), calls=%async_computation.1 | async-start | bytes 2162688 | tf_op jit(solution)/shard_map/all_gather | solution.py:50
  8.0 6.5 %collective-permute-start = (bf16[3,2,128]{2,1,0:T(2,128)(2,1)S(1)}, bf16[3,2,128]{2,1,0:T(2,128)(2,1)S(1)}, u32[]{:S(2)}, u32[]{:S(2)}) collective-permute-start(bf16[3,2,128]{2,1,0:T(2,128)(2,1)S(1)} %pad_maximum_fusion.1), channel_id=1, source_target_pairs={{0,32},{32,64},{64,96},{96,128},{128,160},{160,192},{192,224},{224... | collective-permute-start | bytes 4616 | tf_op jit(solution)/shard_map/ppermute | solution.py:14
  79.0 138.0 %all-gather.5.cloned.1.call-start = ((), (), s32[]{:S(2)}) async-start(), calls=%async_computation.2 | async-start | bytes 4456448 | tf_op jit(solution)/shard_map/all_gather | solution.py:67
  79.7 215.3 %reduce-scatter.2.cloned.1.call-start = ((), (), s32[]{:S(2)}) async-start(), calls=%async_computation.3 | async-start | bytes 4456448 | tf_op jit(solution)/shard_map/reduce_scatter | solution.py:88
  174.2 50.2 %copy-start = (bf16[384,4096]{1,0:T(8,128)(2,1)S(1)}, bf16[384,4096]{1,0:T(8,128)(2,1)}, u32[]{:S(2)}) copy-start(bf16[384,4096]{1,0:T(8,128)(2,1)} %gather_fusion.1) | copy-start | bytes 9437188
  217.0 7.5 %copy-start.1 = (bf16[384,256]{1,0:T(8,128)(2,1)S(1)}, bf16[384,256]{1,0:T(8,128)(2,1)}, u32[]{:S(2)}) copy-start(bf16[384,256]{1,0:T(8,128)(2,1)} %gather_fusion.2) | copy-start | bytes 589828
Sparse Core Ops, SparseCore 0:
  79.1 89.2 all-gather.2
  170.5 46.4 all-gather.4
  230.3 64.7 reduce-scatter.1
where the time goes:
time: 304 us
  waiting for transfers between devices  187 us (62%)
  blocking collectives  62.6 us (21%)
  local copies, waits for them, and re-layouts  16.6 us (5%)
  between operations  13.9 us (5%)
  matrix products  13.1 us (4%)
  other arithmetic  5.15 us (2%)
  starting transfers between devices  5.08 us (2%)
    all_gather x1, waiting for transfers between devices, on_device(): gathered = lax.all_gather(normed, 'expert', axis=1, tiled=True)  81.5 us
    psum x1, blocking collectives, on_device(): total = lax.psum(jnp.sum(mixed_f * mixed_f, axis=1), 'expert')  62.6 us
    reduce_scatter x1, waiting for transfers between devices, on_device(): lax.psum_scatter(jnp.einsum('brd,ebrh->deh', columns, masked_grad, prefer...  62.2 us
    all_gather x1, waiting for transfers between devices, on_device(): lax.all_gather(w_proj, 'dp', axis=0, tiled=True)  42.7 us
    dot_general x1, matrix products, on_device(): jnp.einsum('neh,be->bnh', lax.all_gather(w_proj, 'dp', axis=0, tiled=True...  7.48 us
  transfers between devices with their start and end apart: 4, of which 3 were waited for; matrix products, arithmetic and copies ran while one was open for 6% of the time, Pallas kernels for 0%

commit v1 on v0

--- a/solution.py
+++ b/solution.py
@@ -1,3 +1,4 @@
+import functools
 import jax
 import jax.numpy as jnp
 from jax import lax
@@ -6,6 +7,18 @@
 D = 4096
 BLOCK = 128
 epsilon = 1e-06
+
+
+def _try_all_pieces_all(page, comm_axis, ndim_at):
+    inbox = []
+    for _ in range(lax.axis_size(comm_axis)):
+        inbox.append(page)
+    w1 = jnp.concatenate(inbox, axis=ndim_at)
+    formed = lax.all_to_all(w1, comm_axis, ndim_at, ndim_at, tiled=True)
+    return formed
+
+
+pair_gates = functools.partial(_try_all_pieces_all, comm_axis="expert", ndim_at=1)
 
 
 def from_behind(value, axis, steps):
@@ -47,7 +60,7 @@
     total = lax.psum(jnp.sum(mixed_f * mixed_f, axis=1), "expert")
     inv_rms = lax.rsqrt(total / D + epsilon)
     normed = (mixed_f * inv_rms[:, None] * norm_gain.astype(jnp.float32)).astype(jnp.bfloat16)
-    gathered = lax.all_gather(normed, "expert", axis=1, tiled=True)
+    gathered = pair_gates(normed)
     tok_count = gathered.shape[0]
     slots = slot_token[0]
     num_blocks = slots.shape[0] // BLOCK

time: 304 us -> 227 us (0.75)
  the two profiles are of different devices: /device:TPU:29 before, /device:TPU:31 now
where the time goes in v1:
time: 227 us
  waiting for transfers between devices  103 us (45%)
  blocking collectives  59.2 us (26%)
  local copies, waits for them, and re-layouts  17.2 us (8%)
  starting transfers between devices  16.5 us (7%)
  between operations  14.2 us (6%)
  matrix products  13.3 us (6%)
  other arithmetic  3.14 us (1%)
    reduce_scatter x1, waiting for transfers between devices, on_device(): lax.psum_scatter(jnp.einsum('brd,ebrh->deh', columns, masked_grad, prefer...  71.9 us
    psum x1, blocking collectives, on_device(): total = lax.psum(jnp.sum(mixed_f * mixed_f, axis=1), 'expert')  59.2 us
    all_to_all x1, waiting for transfers between devices, _try_all_pieces_all(): formed = lax.all_to_all(w1, comm_axis, ndim_at, ndim_at, tiled=True)  30.7 us
    all_to_all x1, starting transfers between devices, _try_all_pieces_all(): formed = lax.all_to_all(w1, comm_axis, ndim_at, ndim_at, tiled=True)  11.5 us
    dot_general x1, matrix products, on_device(): jnp.einsum('neh,be->bnh', lax.all_gather(w_proj, 'dp', axis=0, tiled=True...  7.6 us
    ppermute x1, starting transfers between devices, from_behind(): lax.ppermute(value, axis, [(source, source + steps) for source in range(l...  4.96 us
  transfers between devices with their start and end apart: 4, of which 2 were waited for; matrix products, arithmetic and copies ran while one was open for 8% of the time, Pallas kernels for 0%

profile of v1, /device:TPU:31, one launch (start us, length us, event | category | flops | bytes accessed | tf_op | source)
XLA Modules:
  0.0 226.8 jit_solution(937960029635959912)
XLA Ops:
  7.2 0.7 all-gather.2.cloned.1.call-update
  7.9 0.7 pad_maximum_fusion.1
  8.6 5.0 %collective-permute-start = (bf16[3,2,128]{2,1,0:T(2,128)(2,1)S(1)}, bf16[3,2,128]{2,1,0:T(2,128)(2,1)S(1)}, u32[]{:S(2)}, u32[]{:S(2)}) collective-permute-start(bf16[3,2,128]{2,1,0:T(2,128)(2,1)S(1)} %pad_maximum_fusion.1), channel_id=1, source_target_pairs={{0,32},{32,64},{64,96},{96,128},{128,160},{160,192},{192,224},{224... | collective-permute-start | bytes 4616 | tf_op jit(solution)/shard_map/ppermute | solution.py:27
  13.6 0.8 fusion.29
  14.4 0.7 convert_element_type.164
  15.1 0.9 maximum_convert_fusion
  16.3 59.2 %psum.7 = f32[256]{0:T(256)S(1)} all-reduce(f32[256]{0:T(256)S(1)} %get-tuple-element.10), channel_id=1, replica_groups=mesh['dp'=16,'expert'=32] {'expert'}, use_global_device_ids=true, to_apply=%region_1.0 | all-reduce | flops 256 | bytes 2048 | tf_op jit(solution)/shard_map/psum | solution.py:60
  75.7 1.8 concatenate.18
  77.5 11.5 %all-to-all-start = ((bf16[256,32,128]{2,0,1:T(8,128)(2,1)}), bf16[256,32,128]{2,0,1:T(8,128)(2,1)S(1)}, u32[]{:S(2)}, u32[]{:S(2)}) async-start(bf16[256,32,128]{2,0,1:T(8,128)(2,1)} %concatenate.18), calls=%async_computation | async-start | bytes 4194304 | tf_op jit(solution)/shard_map/all_to_all | solution.py:17
  89.1 2.8 %gather_fusion = f32[384]{0:T(512)S(1)} fusion(f32[257]{0:T(512)S(1)} %pad_maximum_fusion, s32[1024]{0:T(1024)S(1)} %pad_clamp_fusion), kind=kCustom, calls=%fused_computation | custom fusion | bytes 4608 | tf_op jit(solution)/shard_map/gather | solution.py:86
  91.9 2.6 %gather_fusion.2 = bf16[384,256]{1,0:T(8,128)(2,1)} fusion(bf16[257,256]{1,0:T(8,128)(2,1)S(1)} %concatenate.20, s32[1024]{0:T(1024)S(1)} %pad_clamp_fusion), kind=kCustom, calls=%fused_computation.2 | custom fusion | bytes 394752 | tf_op jit(solution)/shard_map/gather | solution.py:92
  94.5 0.2 reduce-window.8
  94.8 30.7 %all-to-all-done = bf16[256,32,128]{2,0,1:T(8,128)(2,1)S(1)} async-done(((bf16[256,32,128]{2,0,1:T(8,128)(2,1)}), bf16[256,32,128]{2,0,1:T(8,128)(2,1)S(1)}, u32[]{:S(2)}, u32[]{:S(2)}) %all-to-all-start) | async-done | bytes 2097184 | tf_op jit(solution)/shard_map/all_to_all | solution.py:17
  125.5 0.3 copy_bitcast_fusion
  125.8 0.2 concatenate.19
  126.0 4.1 %gather_fusion.1 = bf16[384,4096]{1,0:T(8,128)(2,1)} fusion(bf16[257,4096]{1,0:T(8,128)(2,1)S(1)} %concatenate.19, s32[1024]{0:T(1024)S(1)} %pad_clamp_fusion), kind=kCustom, calls=%fused_computation.1 | custom fusion | bytes 6292992 | tf_op jit(solution)/shard_map/gather | solution.py:71
  130.1 7.6 %convolution_convert_fusion = bf16[3,4096,256]{2,0,1:T(4,128)(2,1)S(1)} fusion(bf16[4096,2,256]{2,1,0:T(2,128)(2,1)} %all-gather.2.cloned.1.call-done, s32[3]{0:T(128)S(1)} %broadcast_minimum_fusion), kind=kOutput, calls=%fused_computation.5 | convolution fusion | flops 15728646 | bytes 10485772 | tf_op jit(solution)/shard_map/neh,be->bnh/dot_general | solution.py:78
  137.7 1.3 fusion.6
  139.0 4.4 %bitcast_convert_fusion = bf16[4096,2,256]{2,0,1:T(8,128)(2,1)} fusion(bf16[3,128,4096,1]{2,1,0,3:T(8,128)(2,1)S(1)} %bitcast.55, bf16[2,3]{1,0:T(2,128)(2,1)S(1)} %compare_convert_fusion, bf16[3,128,256]{2,1,0:T(8,128)(2,1)S(1)} %get-tuple-element.15), kind=kOutput, calls=%fused_computation.4 | convolution fusion | flops 1613496320 | bytes 7536652 | tf_op jit(solution)/shard_map/brd,ebrh->deh/dot_general | solution.py:102
  143.4 0.1 fusion.8
  143.6 1.9 scatter_custom_fusion
  145.4 0.7 slice.56
  146.1 71.9 %reduce-scatter.2.cloned.1.call-done = bf16[256,2,256]{2,0,1:T(8,128)(2,1)} async-done(((bf16[4096,2,256]{2,0,1:T(8,128)(2,1)}), bf16[256,2,256]{2,0,1:T(8,128)(2,1)}) %reduce-scatter.2.cloned.1.call-update) | async-done | bytes 262160 | tf_op jit(solution)/shard_map/reduce_scatter | solution.py:101
  218.0 2.0 copy.23
  (32 shorter events, 0.7 us)
Async XLA Ops:
  7.2 122.9 %all-gather.2.cloned.1.call-start = ((), (), s32[]{:S(2)}) async-start(), calls=%async_computation.2 | async-start | bytes 4456448 | tf_op jit(solution)/shard_map/all_gather | solution.py:80
  8.6 6.5 %collective-permute-start = (bf16[3,2,128]{2,1,0:T(2,128)(2,1)S(1)}, bf16[3,2,128]{2,1,0:T(2,128)(2,1)S(1)}, u32[]{:S(2)}, u32[]{:S(2)}) collective-permute-start(bf16[3,2,128]{2,1,0:T(2,128)(2,1)S(1)} %pad_maximum_fusion.1), channel_id=1, source_target_pairs={{0,32},{32,64},{64,96},{96,128},{128,160},{160,192},{192,224},{224... | collective-permute-start | bytes 4616 | tf_op jit(solution)/shard_map/ppermute | solution.py:27
  75.6 13.4 %copy-start.4 = (f32[256]{0:T(256)S(1)}, f32[256]{0:T(256)}, u32[]{:S(2)}) copy-start(f32[256]{0:T(256)} %param.17) | copy-start | bytes 3076
  75.6 13.4 %copy-start.3 = (s32[1,384]{1,0:T(1,128)S(1)}, s32[1,384]{1,0:T(1,128)}, u32[]{:S(2)}) copy-start(s32[1,384]{1,0:T(1,128)} %param.15) | copy-start | bytes 4612
  77.5 14.4 %copy-start.2 = (bf16[256,256]{1,0:T(8,128)(2,1)S(1)}, bf16[256,256]{1,0:T(8,128)(2,1)}, u32[]{:S(2)}) copy-start(bf16[256,256]{1,0:T(8,128)(2,1)} %param.19) | copy-start | bytes 393220
  77.5 17.0 %copy-start.5 = (s32[1,2]{1,0:T(1,128)S(1)}, s32[1,2]{1,0:T(1,128)}, u32[]{:S(2)}) copy-start(s32[1,2]{1,0:T(1,128)} %param.16) | copy-start | bytes 28
  77.5 48.0 %all-to-all-start = ((bf16[256,32,128]{2,0,1:T(8,128)(2,1)}), bf16[256,32,128]{2,0,1:T(8,128)(2,1)S(1)}, u32[]{:S(2)}, u32[]{:S(2)}) async-start(bf16[256,32,128]{2,0,1:T(8,128)(2,1)} %concatenate.18), calls=%async_computation | async-start | bytes 4194304 | tf_op jit(solution)/shard_map/all_to_all | solution.py:17
  88.9 129.0 %reduce-scatter.2.cloned.1.call-start = ((), (), s32[]{:S(2)}) async-start(), calls=%async_computation.3 | async-start | bytes 4456448 | tf_op jit(solution)/shard_map/reduce_scatter | solution.py:101
  130.1 7.6 %copy-start = (bf16[384,4096]{1,0:T(8,128)(2,1)S(1)}, bf16[384,4096]{1,0:T(8,128)(2,1)}, u32[]{:S(2)}) copy-start(bf16[384,4096]{1,0:T(8,128)(2,1)} %gather_fusion.1) | copy-start | bytes 9437188
  130.1 7.6 %copy-start.1 = (bf16[384,256]{1,0:T(8,128)(2,1)S(1)}, bf16[384,256]{1,0:T(8,128)(2,1)}, u32[]{:S(2)}) copy-start(bf16[384,256]{1,0:T(8,128)(2,1)} %gather_fusion.2) | copy-start | bytes 589828
Sparse Core Ops, SparseCore 0:
  10.1 48.7 all-gather.1
  143.5 74.4 reduce-scatter.1
